TPU v7x, 128 devices: a whole 4x4x4 slice. The times are simulated.
128 devices in a mesh: replica: 8 (over y_hi, z), tp: 16 (over x, y_lo, core).
Axes of the slice: x: 4, y: 4 (y_hi: 2, y_lo: 2; y = y_hi * 2 + y_lo), z: 4, core: 2. Of those that a mesh axis runs over, the one named last changes fastest.
Arguments:
- changed_layers: int32 [4], replicated, may hold values from 0 to 3, each once
- bucket_owner: int32 [16], replicated, may hold values from 0 to 15, each once
- query_up: bfloat16 [4, 1536, 16384], P(None, ('replica', 'tp')), may hold values from -0.5 to 0.5
- key_up: bfloat16 [4, 512, 16384], P(None, ('replica', 'tp')), may hold values from -0.5 to 0.5
- query_latent: bfloat16 [6144, 1536], P('replica'), may hold values from -1.796875 to 1.796875
Outputs:
- absorbed: bfloat16 [1, 128, 1536, 512], P(None, 'tp')
- query_absorbed: bfloat16 [1, 6144, 128, 512], P(None, 'replica', 'tp')
Inputs may be any that keep to these rules, and one draw needn't show every extreme that they name: `changed_layers`: distinct held layers. `bucket_owner`: each tp position owns exactly one bucket.
All inputs are finite; a program needn't handle non-finite values.
Results may differ from a plain program's by a relative error of at most 0.0049.
Values may be sent and summed in bfloat16 or wider, within the bound.
A program may use at most 128 MiB of HBM per device.

v0:
```python
import jax
import jax.numpy as jnp
from jax import lax
from jax.sharding import PartitionSpec as P

HEAD_NOPE = 128


def absorb_rows(query_rows, key_full):
    local_heads = query_rows.shape[1] // HEAD_NOPE
    query_heads = query_rows.reshape(query_rows.shape[0], local_heads, HEAD_NOPE).transpose(1, 0, 2)
    key_heads = key_full.reshape(key_full.shape[0], local_heads, HEAD_NOPE).transpose(1, 0, 2)

    def one_head(pair):
        return lax.dot_general(
            pair[0], pair[1], (((1,), (1,)), ((), ())), preferred_element_type=jnp.float32
        ).astype(jnp.bfloat16)

    return lax.map(one_head, (query_heads, key_heads))


def owner_order_outer(received, bucket_owner, group_size, replica_count):
    cols = received.shape[1]
    blocks = received.reshape(
        group_size, replica_count, received.shape[0] // (group_size * replica_count), cols
    )
    blocks = jnp.take(blocks, bucket_owner, axis=0).transpose(1, 0, 2, 3)
    return blocks.reshape(received.shape[0], cols)


def shards(changed_layers, bucket_owner, query_up, key_up, query_latent):
    group_size = lax.axis_size("tp")
    replica_count = lax.axis_size("replica")
    layer_id = changed_layers[0]
    up_query = lax.dynamic_index_in_dim(query_up, layer_id, 0, keepdims=False)
    up_key = lax.dynamic_index_in_dim(key_up, layer_id, 0, keepdims=False)
    query_all = lax.all_gather(up_query, "replica", axis=0, tiled=True)
    key_all = lax.all_gather(up_key, "replica", axis=0, tiled=True)
    query_mine = lax.all_to_all(query_all, "tp", split_axis=1, concat_axis=0, tiled=True)
    key_mine = lax.all_to_all(key_all, "tp", split_axis=1, concat_axis=0, tiled=True)
    query_full = owner_order_outer(query_mine, bucket_owner, group_size, replica_count)
    key_full = owner_order_outer(key_mine, bucket_owner, group_size, replica_count)
    absorbed = absorb_rows(query_full, key_full)
    projected = jnp.einsum(
        "rq,hqk->rhk", query_latent, absorbed, preferred_element_type=jnp.float32
    ).astype(jnp.bfloat16)
    absorbed_all = [absorbed]
    queries_all = [projected]
    return (jnp.stack(absorbed_all), jnp.stack(queries_all))


def solution(mesh):
    in_specs = (
        P(),
        P(),
        P(None, ("replica", "tp"), None),
        P(None, ("replica", "tp"), None),
        P("replica", None),
    )
    out_specs = (P(None, "tp", None, None), P(None, "replica", "tp", None))
    return jax.shard_map(shards, mesh=mesh, in_specs=in_specs, out_specs=out_specs, check_vma=False)
```

profile of v0, /device:TPU:0, one launch (start us, length us, event | category | flops | bytes accessed | tf_op | source)
XLA Modules:
  0.0 317.3 jit_solution(16481890702427534770)
XLA Ops:
  7.2 0.0 copy-start
  7.2 0.0 all-gather.7.cloned.1.call-start
  9.3 1.0 constant_dynamic-slice_fusion
  10.3 0.9 copy.50
  11.2 0.0 all-gather.7.cloned.1.call-update
  11.2 0.0 all-gather.5.cloned.1.call-start
  11.3 3.2 %constant_dynamic-slice_fusion.1 = bf16[1,12,16384]{2,0,1:T(2,128)(2,1)} fusion(bf16[4,12,16384]{2,0,1:T(4,128)(2,1)} %param.9, s32[]{:T(128)S(6)} %select_n.30), kind=kLoop, calls=%fused_computation.20 | loop fusion | bytes 786436 | tf_op jit(solution)/shard_map/jit(dynamic_index_in_dim)/dynamic_slice | solution.py:35
  14.5 0.0 all-gather.5.cloned.1.call-update
  14.5 53.5 %all-gather.7.cloned.1.call-done = bf16[1,32,16384]{2,0,1:T(2,128)(2,1)} async-done(((bf16[1,4,16384]{2,0,1:T(2,128)(2,1)}), bf16[1,32,16384]{2,0,1:T(2,128)(2,1)}) %all-gather.7.cloned.1.call-update) | async-done | bytes 1048592 | tf_op jit(solution)/shard_map/all_gather | solution.py:38
  68.0 7.8 %reduce.1 = bf16[32,16384]{1,0:T(8,128)(2,1)S(1)} reduce(bf16[1,32,16384]{2,0,1:T(2,128)(2,1)} %all-gather.7.cloned.1.call-done, bf16[]{:T(256)} %constant.53), dimensions={0}, to_apply=%all-gather.1.reduce_sub_computation | reduce | bytes 2097154 | tf_op jit(solution)/shard_map/all_gather | solution.py:38
  75.8 1.1 copy.56
  76.8 4.4 %all-to-all-start.1 = ((bf16[32,16,1024]{2,0,1:T(8,128)(2,1)}), bf16[32,16,1024]{2,0,1:T(8,128)(2,1)S(1)}, u32[]{:S(2)}, u32[]{:S(2)}) async-start(bf16[32,16,1024]{2,0,1:T(8,128)(2,1)} %bitcast.51), calls=%async_computation.1 | async-start | bytes 2097152 | tf_op jit(solution)/shard_map/all_to_all | solution.py:40
  81.2 87.7 %all-gather.5.cloned.1.call-done = bf16[1,96,16384]{2,0,1:T(2,128)(2,1)} async-done(((bf16[1,12,16384]{2,0,1:T(2,128)(2,1)}), bf16[1,96,16384]{2,0,1:T(2,128)(2,1)}) %all-gather.5.cloned.1.call-update) | async-done | bytes 3145744 | tf_op jit(solution)/shard_map/all_gather | solution.py:37
  168.9 19.9 %reduce = bf16[96,16384]{1,0:T(8,128)(2,1)} reduce(bf16[1,96,16384]{2,0,1:T(2,128)(2,1)} %all-gather.5.cloned.1.call-done, bf16[]{:T(256)} %constant.53), dimensions={0}, to_apply=%all-gather.reduce_sub_computation | reduce | bytes 6291458 | tf_op jit(solution)/shard_map/all_gather | solution.py:37
  188.8 4.0 %copy.55 = bf16[12,16,8,1024]{3,2,0,1:T(8,128)(2,1)} copy(bf16[12,16,8,1024]{3,2,1,0:T(8,128)(2,1)} %bitcast.50) | data formatting | bytes 6291456 | tf_op jit(solution)/shard_map/all_to_all | solution.py:39
  192.8 0.0 all-to-all-done.1
  192.9 0.0 copy-start.2
  192.9 4.8 %all-to-all-start = ((bf16[96,16,1024]{2,0,1:T(8,128)(2,1)}), bf16[96,16,1024]{2,0,1:T(8,128)(2,1)}, u32[]{:S(2)}, u32[]{:S(2)}) async-start(bf16[96,16,1024]{2,0,1:T(8,128)(2,1)} %bitcast.48), calls=%async_computation | async-start | bytes 6291456 | tf_op jit(solution)/shard_map/all_to_all | solution.py:39
  197.7 0.0 copy-done.2
  197.7 0.6 copy.42
  198.3 1.5 copy.43
  199.8 1.8 gather_fusion.1
  201.7 0.2 select_bitcast_fusion.1
  201.9 0.8 copy.44
  202.7 1.2 reshape_reshape.7
  203.9 1.4 copy.46
  205.3 31.4 %all-to-all-done = bf16[96,16,1024]{2,0,1:T(8,128)(2,1)} async-done(((bf16[96,16,1024]{2,0,1:T(8,128)(2,1)}), bf16[96,16,1024]{2,0,1:T(8,128)(2,1)}, u32[]{:S(2)}, u32[]{:S(2)}) %all-to-all-start) | async-done | bytes 3145760 | tf_op jit(solution)/shard_map/all_to_all | solution.py:39
  236.7 3.6 %copy.37 = bf16[96,16,1024]{2,1,0:T(8,128)(2,1)S(1)} copy(bf16[96,16,1024]{2,0,1:T(8,128)(2,1)} %all-to-all-done) | data formatting | bytes 6291456 | tf_op jit(solution)/shard_map/all_to_all | solution.py:39
  240.3 3.4 %copy.38 = bf16[16,8,12,1024]{3,1,2,0:T(8,128)(2,1)} copy(bf16[16,8,12,1024]{3,0,2,1:T(8,128)(2,1)S(1)} %bitcast.49) | data formatting | bytes 6291456 | tf_op jit(solution)/shard_map/reshape | solution.py:24
  243.7 4.3 %gather_fusion = bf16[16,8,12,1024]{3,1,2,0:T(8,128)(2,1)} fusion(bf16[16,8,12,1024]{3,1,2,0:T(8,128)(2,1)} %copy.38, s32[1024]{0:T(1024)S(1)} %pad_clamp_fusion), kind=kCustom, calls=%fused_computation | custom fusion | bytes 6291520 | tf_op jit(solution)/shard_map/jit(_take)/gather | solution.py:27
  247.9 2.3 select_bitcast_fusion
  250.2 3.8 %copy.39 = bf16[8,16,12,1024]{3,2,1,0:T(8,128)(2,1)} copy(bf16[8,16,12,1024]{3,0,2,1:T(8,128)(2,1)S(1)} %select_bitcast_fusion) | data formatting | bytes 6291456 | tf_op jit(solution)/shard_map/jit(_take)/select_n | solution.py:27
  254.0 6.9 %reshape_reshape.6 = bf16[1536,8,128]{2,1,0:T(8,128)(2,1)} reshape(bf16[8,16,12,1024]{3,2,1,0:T(8,128)(2,1)} %copy.39) | data formatting | bytes 6291456 | tf_op jit(solution)/shard_map/reshape;reshape | solution.py:11
  260.9 4.0 %copy.45 = bf16[8,1536,128]{2,1,0:T(8,128)(2,1)} copy(bf16[8,1536,128]{2,0,1:T(8,128)(2,1)} %bitcast.47) | data formatting | bytes 6291456 | tf_op jit(solution)/shard_map/while | solution.py:19
  264.9 21.7 %while.10 = (s32[]{:T(128)}, bf16[8,1536,512]{2,1,0:T(8,128)(2,1)}, bf16[8,1536,128]{2,1,0:T(8,128)(2,1)}, bf16[8,512,128]{2,1,0:T(8,128)(2,1)S(1)}, s32[]{:T(128)}) while((s32[]{:T(128)}, bf16[8,1536,512]{2,1,0:T(8,128)(2,1)}, bf16[8,1536,128]{2,1,0:T(8,128)(2,1)}, bf16[8,512,128]{2,1,0:T(8,128)(2,1)S(1)}, s32[]{:T(128)}) %tuple.31), condition=%wide.region_1.2_spmd, body=%wide.region_0.1_spmd.sunk | while | flops 202113024 | bytes 2098757 | solution.py:19
  264.9 2.7 fusion.14
  267.6 2.7 fusion.14
  270.3 2.7 fusion.14
  273.0 2.7 fusion.14
  275.7 2.7 fusion.14
  278.4 2.7 fusion.14
  281.1 2.7 fusion.14
  283.8 2.7 fusion.14
  286.6 0.0 copy-done
  286.6 14.7 %convert_bitcast_fusion = bf16[1,768,8,512]{1,3,2,0:T(8,128)(2,1)} fusion(bf16[8,1536,512]{2,1,0:T(8,128)(2,1)} %get-tuple-element.24, bf16[768,1536]{1,0:T(8,128)(2,1)S(1)} %copy-done), kind=kOutput, calls=%fused_computation.10 | convolution fusion | flops 9666822144 | bytes 21233664 | tf_op jit(solution)/shard_map/rq,hqk->rhk/dot_general | solution.py:44
  301.3 0.0 copy-start.1
  301.3 9.2 %copy.48 = bf16[1,768,8,512]{3,2,1,0:T(8,128)(2,1)} copy(bf16[1,768,8,512]{1,3,2,0:T(8,128)(2,1)} %convert_bitcast_fusion) | data formatting | bytes 12582912
  310.5 0.0 copy-done.1
  (4 shorter events, 0.0 us)
Async XLA Ops:
  7.2 279.4 %copy-start = (bf16[768,1536]{1,0:T(8,128)(2,1)S(1)}, bf16[768,1536]{1,0:T(8,128)(2,1)}, u32[]{:S(2)}) copy-start(bf16[768,1536]{1,0:T(8,128)(2,1)} %param.11) | copy-start | bytes 7077892
  7.2 60.8 %all-gather.7.cloned.1.call-start = ((), (), s32[]{:S(2)}) async-start(), calls=%async_computation.3 | async-start | bytes 2359296 | tf_op jit(solution)/shard_map/all_gather | solution.py:38
  11.2 157.7 %all-gather.5.cloned.1.call-start = ((), (), s32[]{:S(2)}) async-start(), calls=%async_computation.2 | async-start | bytes 7077888 | tf_op jit(solution)/shard_map/all_gather | solution.py:37
  76.8 116.0 %all-to-all-start.1 = ((bf16[32,16,1024]{2,0,1:T(8,128)(2,1)}), bf16[32,16,1024]{2,0,1:T(8,128)(2,1)S(1)}, u32[]{:S(2)}, u32[]{:S(2)}) async-start(bf16[32,16,1024]{2,0,1:T(8,128)(2,1)} %bitcast.51), calls=%async_computation.1 | async-start | bytes 2097152 | tf_op jit(solution)/shard_map/all_to_all | solution.py:40
  192.9 4.8 %copy-start.2 = (s32[16]{0:T(128)S(1)}, s32[16]{0:T(128)}, u32[]{:S(2)}) copy-start(s32[16]{0:T(128)} %param.8) | copy-start | bytes 196
  192.9 43.8 %all-to-all-start = ((bf16[96,16,1024]{2,0,1:T(8,128)(2,1)}), bf16[96,16,1024]{2,0,1:T(8,128)(2,1)}, u32[]{:S(2)}, u32[]{:S(2)}) async-start(bf16[96,16,1024]{2,0,1:T(8,128)(2,1)} %bitcast.48), calls=%async_computation | async-start | bytes 6291456 | tf_op jit(solution)/shard_map/all_to_all | solution.py:39
  301.3 9.2 %copy-start.1 = (bf16[768,1536]{1,0:T(8,128)(2,1)S(1)}, bf16[768,1536]{1,0:T(8,128)(2,1)}, u32[]{:S(2)}) copy-start(bf16[768,1536]{1,0:T(8,128)(2,1)} %param.11) | copy-start | bytes 7077892
Sparse Core Ops, SparseCore 0:
  11.3 56.6 all-gather.6
  70.9 98.0 all-gather.4
where the time goes:
time: 323 us; the launch traced here: 317 us
  waiting for transfers between devices  173 us (54%)
  local copies, waits for them, and re-layouts  52.7 us (16%)
  matrix products  36.4 us (11%)
  other arithmetic  30.1 us (9%)
  between operations  16.2 us (5%)
  starting transfers between devices  9.25 us (3%)
    all_gather x1, waiting for transfers between devices, shards(): query_all = lax.all_gather(up_query, 'replica', axis=0, tiled=True)  87.7 us
    all_gather x1, waiting for transfers between devices, shards(): key_all = lax.all_gather(up_key, 'replica', axis=0, tiled=True)  53.5 us
    all_to_all x1, waiting for transfers between devices, shards(): lax.all_to_all(query_all, 'tp', split_axis=1, concat_axis=0, tiled=True)  31.4 us
    dot_general x8, matrix products, one_head(): lax.dot_general(pair[0], pair[1], (((1,), (1,)), ((), ())), preferred_ele...  21.7 us
    all_gather x1, other arithmetic, shards(): query_all = lax.all_gather(up_query, 'replica', axis=0, tiled=True)  19.9 us
    dot_general x1, matrix products, shards(): jnp.einsum('rq,hqk->rhk', query_latent, absorbed, preferred_element_type=...  14.7 us
    unnamed x8, local copies, waits for them, and re-layouts  10.2 us
    all_gather x1, other arithmetic, shards(): key_all = lax.all_gather(up_key, 'replica', axis=0, tiled=True)  7.77 us
  transfers between devices with their start and end apart: 4, of which 3 were waited for; matrix products, arithmetic and copies ran while one was open for 14% of the time, Pallas kernels for 0%

commit v1 on v0

v1 whole, which is shorter than its diff:
```python
import jax
import jax.numpy as jnp
from jax import lax
from jax.experimental import pallas as pl
from jax.experimental.pallas import tpu as pltpu
from jax.sharding import PartitionSpec as P

MESH = pl.DeviceIdType.MESH
BF16, F32 = jnp.bfloat16, jnp.float32

DX = (0, 1, 3, 2)
EF = ((0, 0), (0, 1), (1, 0), (1, 1))
NEAR = [(dx, e, f) for dx in DX for e, f in EF]
QROWS, KROWS, ROWS = 12, 4, 16
COLS = 1024
LAYERS = 4


def place():
    r, t = lax.axis_index("replica"), lax.axis_index("tp")
    return t // 4, (t // 2) % 2, t % 2, r // 4, r % 4


def flip(bit, by):
    return 1 - bit if by else bit


def relative(dx, e, f, g, dz):
    x, y_lo, c, y_hi, z = place()
    return flip(y_hi, g) * 4 + (z + dz) % 4, (((x + dx) % 4) * 2 + flip(y_lo, e)) * 2 + flip(c, f)


def back(rel):
    return ((4 - rel[0]) % 4,) + tuple(rel[1:])


def number(rel, g):
    return (rel[0] * 4 + rel[1] * 2 + rel[2]) * 2 + g


def selections(owner_ref):
    out = lax.broadcasted_iota(jnp.int32, (256, 256), 0)
    raw = lax.broadcasted_iota(jnp.int32, (256, 256), 1)
    wanted = jnp.zeros((256, 256), jnp.int32)
    for b in range(16):
        start = owner_ref[b] * ROWS
        wanted = jnp.where((out >= b * QROWS) & (out < (b + 1) * QROWS), start + out - b * QROWS, wanted)
        key_from = 16 * QROWS + b * KROWS
        wanted = jnp.where((out >= key_from) & (out < key_from + KROWS), start + QROWS + out - key_from, wanted)
    return jnp.where(raw == wanted, 1.0, 0.0).astype(BF16)


def gather_kernel(layer_ref, owner_ref, q_hbm, k_hbm, lat_hbm, uq_ref, uk_ref, p_ref,
                  qv, kv, lat, mine, held, sel, spread, acc, load_sem, send_sem, recv_sem):
    x, y_lo, c, y_hi, z = place()
    me_r, me_t = relative(0, 0, 0, 0, 0)
    barrier = pltpu.get_barrier_semaphore()
    partners = [relative(*rel, g, 0) for rel in NEAR for g in range(2) if any(rel) or g]
    partners += [relative(0, 0, 0, 0, dz) for dz in (1, 3)]
    for to in partners:
        pl.semaphore_signal(barrier, inc=1, device_id=to, device_id_type=MESH)

    loads = []
    for i, dx in enumerate(DX):
        columns = pl.ds(pl.multiple_of(((x + dx) % 4) * 4 * COLS, 4 * COLS), 4 * COLS)
        loads.append(pltpu.make_async_copy(q_hbm.at[:, :, columns], qv.at[i], load_sem.at[i]))
    load_k = pltpu.make_async_copy(k_hbm, kv, load_sem.at[4])
    load_lat = pltpu.make_async_copy(lat_hbm, lat, load_sem.at[5])
    load_k.start()
    for load in loads:
        load.start()
    load_lat.start()

    layer = layer_ref[0]
    row = lax.broadcasted_iota(jnp.int32, (ROWS, LAYERS * ROWS), 0)
    raw = lax.broadcasted_iota(jnp.int32, (ROWS, LAYERS * ROWS), 1)
    pick = jnp.where(row < QROWS, row * LAYERS + layer, LAYERS * QROWS + layer * KROWS + row - QROWS)
    pick = jnp.where(raw == pick, 1.0, 0.0).astype(BF16)

    def pack(i, e, f):
        dx = DX[i]
        _, to_t = relative(dx, e, f, 0, 0)
        inner = (to_t % 4) * COLS
        from_q = qv[i, :, :, pl.ds(pl.multiple_of(inner, COLS), COLS)].reshape(LAYERS * QROWS, COLS)
        from_k = kv[:, :, pl.ds(pl.multiple_of(to_t * COLS, COLS), COLS)].reshape(LAYERS * KROWS, COLS)
        return jnp.dot(pick, jnp.concatenate([from_q, from_k], 0), preferred_element_type=F32).astype(BF16)

    sends = []

    def send(source, to, there, number_there, dz_there):
        copy = pltpu.make_async_remote_copy(
            src_ref=source, dst_ref=held.at[there[0], there[1]], send_sem=send_sem.at[len(sends)],
            recv_sem=recv_sem.at[dz_there, number_there], device_id=to, device_id_type=MESH)
        copy.start()
        sends.append(copy)

    def arrive(rel, g, dz):
        there = relative(*rel, g, dz)
        block = held.at[there[0], there[1]]
        pltpu.make_async_remote_copy(
            src_ref=block, dst_ref=block, send_sem=send_sem.at[0], recv_sem=recv_sem.at[dz, number(rel, g)],
            device_id=partners[0], device_id_type=MESH).wait_recv()
        return there, block

    def along_z(there, block, rel, g, dz, up):
        to = relative(0, 0, 0, 0, 1 if up else 3)
        send(block, to, there, number(rel, g), (dz + (3 if up else 1)) % 4)

    load_k.wait()
    for i in range(4):
        loads[i].wait()
        for e, f in EF:
            rel = (DX[i], e, f)
            block = pack(i, e, f)
            if any(rel):
                mine[i * 4 + e * 2 + f] = block
            else:
                held[me_r, me_t] = block
        if i == 0:
            pl.semaphore_wait(barrier, len(partners))
            own = held.at[me_r, me_t]
            for up in (True, False):
                along_z((me_r, me_t), own, (0, 0, 0), 0, 0, up)
        for e, f in EF:
            rel = (DX[i], e, f)
            if any(rel):
                send(mine.at[i * 4 + e * 2 + f], relative(*rel, 0, 0), (me_r, me_t), number(back(rel), 0), 0)
    for i in range(4):
        for e, f in EF:
            rel = (DX[i], e, f)
            source = mine.at[i * 4 + e * 2 + f] if any(rel) else own
            send(source, relative(*rel, 1, 0), (me_r, me_t), number(back(rel), 1), 0)

    order = [back(rel) for rel in NEAR]
    for rel in order:
        if any(rel):
            there, block = arrive(rel, 0, 0)
            for up in (True, False):
                along_z(there, block, rel, 0, 0, up)
    for rel in order:
        up = rel[2] == 0
        there, block = arrive(rel, 0, 3 if up else 1)
        along_z(there, block, rel, 0, 3 if up else 1, up)
    for rel in order:
        there, block = arrive(rel, 1, 0)
        for up in (True, False):
            along_z(there, block, rel, 1, 0, up)

    sel[...] = selections(owner_ref)
    load_lat.wait()
    pair_q = sel[0:192, :]
    zero = jnp.zeros((192, 256), BF16)
    pair_q = jnp.concatenate([jnp.concatenate([pair_q, zero], 1), jnp.concatenate([zero, pair_q], 1)], 0)
    for pair in range(4):
        both = jnp.dot(lat[:, pair * 384:(pair + 1) * 384], pair_q, preferred_element_type=F32).astype(BF16)
        spread[2 * pair] = both[:, :256]
        spread[2 * pair + 1] = both[:, 256:]

    def absorb_slab(g, dz, first=False, last=False):
        r, _ = relative(0, 0, 0, g, dz)
        slab = held[r].reshape(256, COLS)
        ordered = jnp.dot(sel[...], slab, preferred_element_type=F32).astype(BF16)
        uq_ref[r] = ordered[:192]
        uk_ref[r] = ordered[192:]
        term = jnp.dot(spread[r], slab, preferred_element_type=F32)
        total = term if first else acc[...] + term
        if last:
            p_ref[...] = total.astype(BF16)
        else:
            acc[...] = total

    absorb_slab(0, 0, first=True)
    for rel in order:
        there, block = arrive(rel, 0, 2)
        send(block, relative(0, 0, 0, 1, 0), there, number(rel, 1), 2)
    absorb_slab(1, 0)
    for dz in (1, 3):
        for rel in order:
            if rel[2] == (1 if dz == 3 else 0):
                arrive(rel, 0, dz)
        absorb_slab(0, dz)
    absorb_slab(0, 2)
    for rel in order:
        arrive(rel, 1, 2)
    absorb_slab(1, 2)
    for dz in (1, 3):
        for rel in order:
            arrive(rel, 1, dz)
        absorb_slab(1, dz, last=dz == 3)
    for copy in sends:
        copy.wait_send()


def gather(layers, owner, query_t, key, latent):
    any_space = pl.BlockSpec(memory_space=pl.ANY)
    smem = pl.BlockSpec(memory_space=pltpu.SMEM)
    vmem = pl.BlockSpec(memory_space=pltpu.VMEM)
    return pl.pallas_call(
        gather_kernel,
        out_shape=(pltpu.VMEM((8, 192, COLS), BF16), pltpu.VMEM((8, 64, COLS), BF16), pltpu.VMEM((768, COLS), BF16)),
        in_specs=[smem, smem, any_space, any_space, any_space],
        out_specs=[vmem, vmem, vmem],
        scratch_shapes=[
            pltpu.VMEM((4, QROWS, LAYERS, 4 * COLS), BF16),
            pltpu.VMEM((LAYERS, KROWS, 16 * COLS), BF16),
            pltpu.VMEM((768, 1536), BF16),
            pltpu.VMEM((16, ROWS, COLS), BF16),
            pltpu.VMEM((8, 16, ROWS, COLS), BF16),
            pltpu.VMEM((256, 256), BF16),
            pltpu.VMEM((8, 768, 256), BF16),
            pltpu.VMEM((768, COLS), F32),
            pltpu.SemaphoreType.DMA((6,)),
            pltpu.SemaphoreType.DMA((127,)),
            pltpu.SemaphoreType.DMA((4, 32)),
        ],
        compiler_params=pltpu.CompilerParams(collective_id=0, has_side_effects=True, vmem_limit_bytes=44 << 20),
    )(layers, owner, query_t, key, latent)


def expand_kernel(uq_ref, uk_ref, p_ref, absorbed_ref, projected_ref, mixed):
    step = pl.program_id(0)
    nt = (((1,), (1,)), ((), ()))
    head = pl.ds(pl.multiple_of(step * 128, 128), 128)
    absorbed_ref[0] = lax.dot_general(uq_ref[:, head], uk_ref[:, head], nt, preferred_element_type=F32).astype(BF16)
    rows = pl.ds(pl.multiple_of(step * 96, 32), 96)
    for h in range(8):
        part = lax.dot_general(p_ref[rows, h * 128:(h + 1) * 128], uk_ref[:, h * 128:(h + 1) * 128], nt, preferred_element_type=F32)
        for lane in range(4):
            mixed[lane, pl.ds(h, 96, stride=8), :] = part[:, lane * 128:(lane + 1) * 128]
    for lane in range(4):
        projected_ref[:, :, lane * 128:(lane + 1) * 128] = mixed[lane].reshape(96, 8, 128).astype(BF16)


def expand(uq, uk, p):
    vmem = pl.BlockSpec(memory_space=pltpu.VMEM)
    return pl.pallas_call(
        expand_kernel,
        grid=(8,),
        out_shape=(jax.ShapeDtypeStruct((8, 1536, 512), BF16), jax.ShapeDtypeStruct((768, 8, 512), BF16)),
        in_specs=[vmem, vmem, vmem],
        out_specs=[pl.BlockSpec((1, 1536, 512), lambda i: (i, 0, 0)), pl.BlockSpec((96, 8, 512), lambda i: (i, 0, 0))],
        scratch_shapes=[pltpu.VMEM((4, 768, 128), F32)],
        compiler_params=pltpu.CompilerParams(vmem_limit_bytes=32 << 20),
    )(uq, uk, p)


def shards(changed_layers, bucket_owner, query_up, key_up, query_latent):
    uq, uk, p = gather(changed_layers, bucket_owner, query_up.transpose(1, 0, 2), key_up, query_latent)
    absorbed, projected = expand(uq.reshape(1536, COLS), uk.reshape(512, COLS), p)
    return absorbed[None], projected[None]


def solution(mesh):
    in_specs = (
        P(),
        P(),
        P(None, ("replica", "tp"), None),
        P(None, ("replica", "tp"), None),
        P("replica", None),
    )
    out_specs = (P(None, "tp", None, None), P(None, "replica", "tp", None))
    return jax.shard_map(shards, mesh=mesh, in_specs=in_specs, out_specs=out_specs, check_vma=False)
```

time: 323 us -> 67.9 us (0.21)
  the two profiles are of different devices: /device:TPU:0 before, /device:TPU:36 now
where the time goes in v1:
time: 67.9 us; the launch traced here: 67.7 us
  Pallas kernels  61.6 us (91%)
  local copies, waits for them, and re-layouts  5.42 us (8%)
    pallas_call x1, Pallas kernels, gather(): pl.pallas_call(gather_kernel, out_shape=(pltpu.VMEM((8, 192, COLS), BF16)...  51 us
    pallas_call x1, Pallas kernels, expand(): pl.pallas_call(expand_kernel, grid=(8,), out_shape=(jax.ShapeDtypeStruct(...  10.6 us
    unnamed x10, local copies, waits for them, and re-layouts  5.42 us

profile of v1, /device:TPU:36, one launch (start us, length us, event | category | flops | bytes accessed | tf_op | source)
XLA Modules:
  0.0 67.7 jit_solution(15186106102646073314)
XLA Ops:
  0.6 0.0 copy-start
  0.6 1.7 %copy-done = bf16[768,1536]{1,0:T(8,128)(2,1)S(1)} copy-done((bf16[768,1536]{1,0:T(8,128)(2,1)S(1)}, bf16[768,1536]{1,0:T(8,128)(2,1)}, u32[]{:S(2)}) %copy-start) | copy-done | bytes 2359320
  2.3 0.0 copy-start.1
  2.3 1.4 %copy-done.1 = bf16[4,12,16384]{2,0,1:T(4,128)(2,1)S(1)} copy-done((bf16[4,12,16384]{2,0,1:T(4,128)(2,1)S(1)}, bf16[4,12,16384]{2,0,1:T(4,128)(2,1)}, u32[]{:S(2)}) %copy-start.1) | copy-done | bytes 1572888
  3.7 0.0 copy-start.2
  3.7 1.0 %copy-done.2 = bf16[4,4,16384]{2,1,0:T(4,128)(2,1)S(1)} copy-done((bf16[4,4,16384]{2,1,0:T(4,128)(2,1)S(1)}, bf16[4,4,16384]{2,1,0:T(4,128)(2,1)}, u32[]{:S(2)}) %copy-start.2) | copy-done | bytes 524312
  4.7 0.0 copy-start.3
  4.8 0.7 copy-done.3
  5.4 0.0 copy-start.4
  5.4 0.7 copy-done.4
  6.1 51.0 %shard_map.68 = (bf16[8,192,1024]{2,1,0:T(8,128)(2,1)S(1)}, bf16[8,64,1024]{2,1,0:T(8,128)(2,1)S(1)}, bf16[768,1024]{1,0:T(8,128)(2,1)S(1)}) custom-call(s32[4]{0:T(128)S(1)} %copy-done.3, s32[16]{0:T(128)S(1)} %copy-done.4, bf16[12,4,16384]{2,1,0:T(4,128)(2,1)S(1)} %bitcast.6, bf16[4,4,16384]{2,1,0:T(4,128)(2,1)S(1)} %copy-done.2, bf16[768,1536]{1,0:T(8,128)(2,1)S(1)} %copy-done), custom_call_target="tpu_custom_call" | custom-call | tf_op jit(solution)/shard_map/pallas_call | solution.py:198
  57.1 10.6 %shard_map.69 = (bf16[8,1536,512]{2,1,0:T(8,128)(2,1)}, bf16[768,8,512]{2,1,0:T(8,128)(2,1)}) custom-call(bf16[1536,1024]{1,0:T(8,128)(2,1)S(1)} %bitcast.5, bf16[512,1024]{1,0:T(8,128)(2,1)S(1)} %bitcast.7, bf16[768,1024]{1,0:T(8,128)(2,1)S(1)} %get-tuple-element.9.p_ref), custom_call_target="tpu_custom_call" | custom-call | tf_op jit(solution)/shard_map/pallas_call | solution.py:236
Async XLA Ops:
  0.6 1.7 %copy-start = (bf16[768,1536]{1,0:T(8,128)(2,1)S(1)}, bf16[768,1536]{1,0:T(8,128)(2,1)}, u32[]{:S(2)}) copy-start(bf16[768,1536]{1,0:T(8,128)(2,1)} %lat_hbm.1) | copy-start | bytes 7077892
  2.3 1.4 %copy-start.1 = (bf16[4,12,16384]{2,0,1:T(4,128)(2,1)S(1)}, bf16[4,12,16384]{2,0,1:T(4,128)(2,1)}, u32[]{:S(2)}) copy-start(bf16[4,12,16384]{2,0,1:T(4,128)(2,1)} %param.7) | copy-start | bytes 4718596
  3.7 1.0 %copy-start.2 = (bf16[4,4,16384]{2,1,0:T(4,128)(2,1)S(1)}, bf16[4,4,16384]{2,1,0:T(4,128)(2,1)}, u32[]{:S(2)}) copy-start(bf16[4,4,16384]{2,1,0:T(4,128)(2,1)} %k_hbm.1) | copy-start | bytes 1572868
  4.7 0.7 copy-start.3
  5.4 0.7 copy-start.4

commit v2 on v0

v2 whole, which is shorter than its diff:
```python
import jax
import jax.numpy as jnp
from jax import lax
from jax.experimental import pallas as pl
from jax.experimental.pallas import tpu as pltpu
from jax.sharding import PartitionSpec as P

MESH = pl.DeviceIdType.MESH
BF16, F32 = jnp.bfloat16, jnp.float32

DX = (0, 1, 3, 2)
QROWS, KROWS, LAYERS = 12, 4, 4
COLS, LANES = 1024, 256
QB, KB = 48, 16
HEADS_HERE, HEAD, KEYS, QUERIES, LATENTS = 8, 128, 512, 1536, 768
SLAB = 192


def place():
    r, t = lax.axis_index("replica"), lax.axis_index("tp")
    return t // 4, (t // 2) % 2, t % 2, r // 4, r % 4


def flip(bit, by):
    return 1 - bit if by else bit


def device(dx=0, e=0, f=0, g=0, dz=0):
    x, y_lo, c, y_hi, z = place()
    return flip(y_hi, g) * 4 + (z + dz) % 4, (((x + dx) % 4) * 2 + flip(y_lo, e)) * 2 + flip(c, f)


def steps(value, size, count):
    return sum((value >= size * k).astype(jnp.int32) for k in range(1, count))


def raw_place(owner_ref, bucket):
    found = jnp.zeros_like(bucket)
    for b in range(16):
        t = owner_ref[b]
        found = jnp.where(bucket == b, ((t // 2) % 2) * 8 + (t // 4) * 2 + t % 2, found)
    return found


def one_hot(wanted, width):
    lane = lax.broadcasted_iota(jnp.int32, (wanted.shape[0], width), 1)
    return jnp.where(lane == wanted, 1.0, 0.0).astype(BF16)


def column(size):
    return lax.broadcasted_iota(jnp.int32, (size, 1), 0)


def query_order(owner_ref):
    out = column(4 * SLAB)
    i = steps(out, SLAB, 4)
    within = out - SLAB * i
    bucket = steps(within, QROWS, 16)
    row = within - QROWS * bucket
    p = steps(row, 4, 3)
    return one_hot(raw_place(owner_ref, bucket) * QB + p * 16 + i * 4 + row - 4 * p, 16 * QB)


def key_order(owner_ref):
    out = column(256)
    i = steps(out, 64, 4)
    within = out - 64 * i
    bucket = steps(within, KROWS, 16)
    return one_hot(raw_place(owner_ref, bucket) * KB + i * 4 + within - KROWS * bucket, 256)


def changed_rows(layer):
    out = column(QB + KB)
    p = steps(out, 16, 4)
    i = steps(out - 16 * p, 4, 4)
    j = out - 16 * p - 4 * i
    row = jnp.where(p < 3, (4 * p + j) * LAYERS + layer, QROWS * LAYERS + layer * KROWS + j)
    return one_hot(i * 64 + row, 256)


def gather_kernel(layer_hbm, owner_hbm, q_hbm, k_hbm, lat_hbm, absorbed_ref, uq_ref, ukt_ref, p_ref,
                  layer_ref, owner_ref, qv, kv, lat, mine, side_k, side_q, held_k, held_q, order_k, order_q, lats, uk, uq, acc,
                  load_sem, send_sem, x_sem, k_sem, q_sem):
    x, y_lo, c, y_hi, z = place()
    y = y_hi * 2 + y_lo
    my_place = x * 2 + c
    barrier = pltpu.get_barrier_semaphore()
    partners = [device(dx=dx, f=f) for dx in DX for f in range(2) if dx or f]
    partners += [device(e=e, f=f, g=g, dz=dz) for e, g, dz in ((1, 0, 0), (0, 1, 0), (1, 1, 0), (0, 0, 1), (0, 0, 3)) for f in range(2)]
    for to in partners:
        pl.semaphore_signal(barrier, inc=1, device_id=to, device_id_type=MESH)

    loads = []
    for n, dx in enumerate(DX):
        columns = pl.ds(pl.multiple_of(((x + dx) % 4) * 4 * COLS, 4 * COLS), 4 * COLS)
        loads.append((pltpu.make_async_copy(q_hbm.at[:, :, columns], qv.at[n], load_sem.at[n]),
                      pltpu.make_async_copy(k_hbm.at[:, :, columns], kv.at[n], load_sem.at[4 + n])))
    load_lat = pltpu.make_async_copy(lat_hbm, lat, load_sem.at[8])
    load_layer = pltpu.make_async_copy(layer_hbm, layer_ref, load_sem.at[9])
    load_owner = pltpu.make_async_copy(owner_hbm, owner_ref, load_sem.at[10])
    load_layer.start()
    for pair in loads:
        for load in pair:
            load.start()
    load_owner.start()
    load_lat.start()
    load_layer.wait()
    pick = changed_rows(layer_ref[0])

    sends = []

    def send(source, target, sem, to):
        copy = pltpu.make_async_remote_copy(src_ref=source, dst_ref=target, send_sem=send_sem.at[len(sends)], recv_sem=sem,
                                            device_id=to, device_id_type=MESH)
        copy.start()
        sends.append(copy)

    def arrive(block, sem):
        pltpu.make_async_remote_copy(src_ref=block, dst_ref=block, send_sem=send_sem.at[0], recv_sem=sem,
                                     device_id=partners[0], device_id_type=MESH).wait_recv()

    def row_at(row, dz):
        return (z + dz) % 4, flip(y_hi, row // 2) * 2 + flip(y_lo, row % 2)

    def keys(row, dz):
        at = row_at(row, dz)
        return held_k.at[at[0], at[1]]

    def queries(row, dz, n):
        at = row_at(row, dz)
        return held_q.at[at[0], at[1], pl.ds(((x + DX[n]) % 4) * 2, 2)]

    def send_keys(row, dz, to, row_there, dz_there):
        send(keys(row, dz), keys(row, dz), k_sem.at[dz_there, row_there], to)

    def send_queries(row, dz, n, to, row_there, dz_there):
        send(queries(row, dz, n), queries(row, dz, n), q_sem.at[dz_there, row_there, n], to)

    up, down = device(dz=1), device(dz=3)
    beside, across, beyond = device(e=1), device(g=1), device(e=1, g=1)

    def keys_along_z(row):
        send_keys(row, 0, up, row, 3)
        send_keys(row, 0, down, row, 1)

    def queries_along_z(row, n):
        send_queries(row, 0, n, up, row, 3)
        send_queries(row, 0, n, down, row, 1)

    def keys_along_y():
        send_keys(0, 0, across, 2, 0)
        for to, row in ((beside, 1), (beyond, 3)):
            send(side_k, keys(0, 0), k_sem.at[0, row], to)

    def queries_along_y(n, e):
        if e == 0:
            send_queries(0, 0, n, across, 2, 0)
            return
        for to, row in ((beside, 1), (beyond, 3)):
            send(side_q.at[pl.ds(((x + DX[n]) % 4) * 2, 2)], queries(0, 0, n), q_sem.at[0, row, n], to)

    def x_index(dx, f):
        return dx * 2 + f

    def arrive_x_keys(n, f):
        at = ((x + DX[n]) % 4) * 2 + flip(c, f)
        arrive(held_k.at[z, y, at], x_sem.at[0, 0, x_index(DX[n], f)])
        arrive(side_k.at[at], x_sem.at[1, 0, x_index(DX[n], f)])

    def arrive_x_queries(n, f, e):
        at = ((x + DX[n]) % 4) * 2 + flip(c, f)
        arrive(side_q.at[at] if e else held_q.at[z, y, at], x_sem.at[e, 1, x_index(DX[n], f)])

    def along_x(n, f, e, part):
        to, there = device(dx=DX[n], f=f), x_index((4 - DX[n]) % 4, f)
        source = mine.at[n * 4 + e * 2 + f]
        if part == 0:
            send(source.at[pl.ds(QB, KB)], side_k.at[my_place] if e else held_k.at[z, y, my_place], x_sem.at[e, 0, there], to)
        else:
            send(source.at[pl.ds(0, QB)], side_q.at[my_place] if e else held_q.at[z, y, my_place], x_sem.at[e, 1, there], to)

    for n, dx in enumerate(DX):
        for load in loads[n]:
            load.wait()
        for e in range(2):
            for f in range(2):
                inner = (flip(y_lo, e) * 2 + flip(c, f)) * COLS
                parts = []
                for i in range(4):
                    columns = pl.ds(pl.multiple_of(inner + i * LANES, LANES), LANES)
                    parts.append(qv[n, :, :, columns].reshape(QROWS * LAYERS, LANES))
                    parts.append(kv[n, :, :, columns].reshape(KROWS * LAYERS, LANES))
                block = jnp.dot(pick, jnp.concatenate(parts, 0), preferred_element_type=F32).astype(BF16)
                mine[n * 4 + e * 2 + f] = block
                if not (dx or f):
                    if e:
                        side_k[my_place] = block[QB:]
                    else:
                        held_q[z, y, my_place] = block[:QB]
                        held_k[z, y, my_place] = block[QB:]
        if n == 0:
            pl.semaphore_wait(barrier, len(partners))
            own = held_q.at[z, y, my_place]
            for f in range(2):
                block = mine.at[f, pl.ds(0, QB)]
                send(block, own, q_sem.at[3, 0, 0], device(dz=1, f=f))
                send(block, own, q_sem.at[1, 0, 0], device(dz=3, f=f))
                send(block, own, q_sem.at[0, 2, 0], device(g=1, f=f))
                block = mine.at[2 + f, pl.ds(0, QB)]
                send(block, own, q_sem.at[0, 1, 0], device(e=1, f=f))
                send(block, own, q_sem.at[0, 3, 0], device(e=1, g=1, f=f))
    for n in range(4):
        for f in range(2):
            if DX[n] or f:
                for e in range(2):
                    along_x(n, f, e, 0)
    for e in range(2):
        for n in (1, 2):
            for f in range(2):
                along_x(n, f, e, 1)
    for e in range(2):
        for f in range(2):
            along_x(3, f, e, 1)
    along_x(0, 1, 0, 1)

    def row_zero(n, e):
        for f in range(2):
            arrive_x_queries(n, f, e)
        if e == 0:
            queries_along_z(0, n)
        queries_along_y(n, e)

    def row_on(row, n):
        arrive(queries(row, 0, n), q_sem.at[0, row, n])
        queries_along_z(row, n)

    def onward(row, n):
        dz, to = ((3, up), (1, down))[row]
        arrive(queries(row, dz, n), q_sem.at[dz, row, n])
        send_queries(row, dz, n, to, row, 2)

    def keys_onward(row):
        dz, to = ((3, up), (1, down))[row]
        arrive(keys(row, dz), k_sem.at[dz, row])
        send_keys(row, dz, to, row, 2)

    def slab_index(g, dz):
        return flip(y_hi, g) * 4 + (z + dz) % 4

    def query_slab(g, dz, first=False, last=False, spare=None):
        at_y = flip(y_hi, g) * 2
        r = slab_index(g, dz)
        raw = held_q[(z + dz) % 4, pl.ds(at_y, 2)].reshape(16 * QB, LANES)
        ordered = jnp.dot(order_q[...], raw, preferred_element_type=F32).astype(BF16)
        for i in range(4):
            uq[r, :, i * LANES:(i + 1) * LANES] = ordered[i * SLAB:(i + 1) * SLAB]
        if spare is not None:
            uq_ref[spare] = uq[r]
        term = jnp.dot(lats[r], uq[r], preferred_element_type=F32)
        total = term if first else acc[...] + term
        if last:
            p_ref[...] = total.astype(BF16)
        else:
            acc[...] = total

    def absorb(g, dz):
        r = slab_index(g, dz)
        rows = pl.ds(pl.multiple_of(r * SLAB, 64), SLAB)
        for h in range(HEADS_HERE):
            absorbed_ref[h, rows] = jnp.dot(uq[r, :, h * HEAD:(h + 1) * HEAD], ukt_ref[h], preferred_element_type=F32).astype(BF16)

    def hand_across(row):
        for n in range(4):
            arrive(queries(row, 2, n), q_sem.at[2, row, n])
            send_queries(row, 2, n, across, row + 2, 2)

    load_owner.wait()
    order_k[...] = key_order(owner_ref)
    order_q[...] = query_order(owner_ref)
    load_lat.wait()
    for r in range(8):
        lats[r] = lat[:, r * SLAB:(r + 1) * SLAB]

    for n in range(4):
        for f in range(2):
            if DX[n] or f:
                arrive_x_keys(n, f)
    keys_along_z(0)
    keys_along_y()
    for e in range(2):
        row_zero(1, e)
        row_zero(2, e)
    row_zero(3, 0)
    row_zero(3, 1)
    for row in (1, 3, 2):
        arrive(keys(row, 0), k_sem.at[0, row])
        keys_along_z(row)
    keys_onward(0)
    keys_onward(1)
    for n in range(4):
        row_on(1, n)
    for n in range(4):
        onward(0, n)
    for row in (0, 1):
        arrive(keys(row, 2), k_sem.at[2, row])
        send_keys(row, 2, across, row + 2, 2)
    for n in range(4):
        onward(1, n)
    arrive_x_queries(0, 1, 0)
    query_slab(0, 0, first=True)
    for n in range(4):
        row_on(3, n)
    hand_across(0)
    for n in range(4):
        row_on(2, n)
    hand_across(1)
    query_slab(1, 0)
    for dz in (1, 3):
        row = 0 if dz == 1 else 1
        for n in range(4):
            arrive(queries(row, dz, n), q_sem.at[dz, row, n])
        query_slab(0, dz)
    for dz in (1, 3):
        for row in range(4):
            if (row, dz) not in ((0, 3), (1, 1)):
                arrive(keys(row, dz), k_sem.at[dz, row])
    for row in (2, 3):
        arrive(keys(row, 2), k_sem.at[2, row])
    for at_z in range(4):
        for at_y in range(2):
            raw = held_k[at_z, 2 * at_y:2 * at_y + 2].reshape(256, LANES)
            ordered = jnp.dot(order_k[...], raw, preferred_element_type=F32).astype(BF16)
            for i in range(4):
                uk[(at_y * 4 + at_z) * 64:(at_y * 4 + at_z) * 64 + 64, i * LANES:(i + 1) * LANES] = ordered[i * 64:(i + 1) * 64]
    for h in range(HEADS_HERE):
        ukt_ref[h] = uk[:, h * HEAD:(h + 1) * HEAD].T
    for g, dz in ((0, 0), (1, 0), (0, 1), (0, 3)):
        absorb(g, dz)
    query_slab(0, 2)
    absorb(0, 2)
    for row in (2, 3):
        for n in range(4):
            arrive(queries(row, 2, n), q_sem.at[2, row, n])
    query_slab(1, 2)
    absorb(1, 2)
    for dz in (1, 3):
        for row in (2, 3):
            for n in range(4):
                arrive(queries(row, dz, n), q_sem.at[dz, row, n])
        query_slab(1, dz, last=dz == 3, spare=dz // 2)
    for copy in sends:
        copy.wait_send()


def gather(layers, owner, query_t, key, latent):
    any_space = pl.BlockSpec(memory_space=pl.ANY)
    vmem = pl.BlockSpec(memory_space=pltpu.VMEM)
    return pl.pallas_call(
        gather_kernel,
        out_shape=(pltpu.VMEM((HEADS_HERE, QUERIES, KEYS), BF16), pltpu.VMEM((2, SLAB, COLS), BF16),
                   pltpu.VMEM((HEADS_HERE, HEAD, KEYS), BF16), pltpu.VMEM((LATENTS, COLS), BF16)),
        in_specs=[any_space] * 5,
        out_specs=[vmem] * 4,
        scratch_shapes=[
            pltpu.SMEM((4,), jnp.int32),
            pltpu.SMEM((16,), jnp.int32),
            pltpu.VMEM((4, QROWS, LAYERS, 4 * COLS), BF16),
            pltpu.VMEM((4, LAYERS, KROWS, 4 * COLS), BF16),
            pltpu.VMEM((LATENTS, QUERIES), BF16),
            pltpu.VMEM((16, QB + KB, LANES), BF16),
            pltpu.VMEM((8, KB, LANES), BF16),
            pltpu.VMEM((8, QB, LANES), BF16),
            pltpu.VMEM((4, 4, 8, KB, LANES), BF16),
            pltpu.VMEM((4, 4, 8, QB, LANES), BF16),
            pltpu.VMEM((256, 256), BF16),
            pltpu.VMEM((4 * SLAB, 16 * QB), BF16),
            pltpu.VMEM((8, LATENTS, SLAB), BF16),
            pltpu.VMEM((KEYS, COLS), BF16),
            pltpu.VMEM((8, SLAB, COLS), BF16),
            pltpu.VMEM((LATENTS, COLS), F32),
            pltpu.SemaphoreType.DMA((11,)),
            pltpu.SemaphoreType.DMA((107,)),
            pltpu.SemaphoreType.DMA((2, 2, 8)),
            pltpu.SemaphoreType.DMA((4, 4)),
            pltpu.SemaphoreType.DMA((4, 4, 4)),
        ],
        compiler_params=pltpu.CompilerParams(collective_id=0, has_side_effects=True, vmem_limit_bytes=43 << 20),
    )(layers, owner, query_t, key, latent)


CHUNK = 192


def expand_kernel(done_ref, uq_ref, ukt_ref, p_ref, absorbed_hbm, projected_hbm, rest, mixed, projected, out_sem, rest_sem, p_sem):
    _, _, _, y_hi, z = place()

    def rows(g, dz):
        return pl.ds(pl.multiple_of((flip(y_hi, g) * 4 + (z + dz) % 4) * SLAB, 64), SLAB)

    copies = []
    for n, (g, dz) in enumerate(((0, 0), (1, 0), (0, 1), (0, 3), (0, 2), (1, 2))):
        copies.append(pltpu.make_async_copy(done_ref.at[:, rows(g, dz)], absorbed_hbm.at[:, rows(g, dz)], out_sem.at[n]))
        copies[-1].start()
    for n in range(LATENTS // CHUNK):
        for h in range(HEADS_HERE):
            part = jnp.dot(p_ref[n * CHUNK:(n + 1) * CHUNK, h * HEAD:(h + 1) * HEAD], ukt_ref[h], preferred_element_type=F32)
            for lane in range(4):
                mixed[lane, pl.ds(h, CHUNK, stride=8), :] = part[:, lane * 128:(lane + 1) * 128]
        for lane in range(4):
            projected[n, :, :, lane * 128:(lane + 1) * 128] = mixed[lane].reshape(CHUNK, 8, 128).astype(BF16)
        copies.append(pltpu.make_async_copy(projected.at[n], projected_hbm.at[pl.ds(n * CHUNK, CHUNK)], p_sem.at[n]))
        copies[-1].start()
        if n < 2:
            for h in range(HEADS_HERE):
                rest[n, h] = jnp.dot(uq_ref[n, :, h * HEAD:(h + 1) * HEAD], ukt_ref[h], preferred_element_type=F32).astype(BF16)
            copies.append(pltpu.make_async_copy(rest.at[n], absorbed_hbm.at[:, rows(1, 1 + 2 * n)], rest_sem.at[n]))
            copies[-1].start()
    for copy in copies:
        copy.wait()


def expand(done, uq, ukt, p):
    vmem = pl.BlockSpec(memory_space=pltpu.VMEM)
    return pl.pallas_call(
        expand_kernel,
        out_shape=(jax.ShapeDtypeStruct((HEADS_HERE, QUERIES, KEYS), BF16), jax.ShapeDtypeStruct((LATENTS, HEADS_HERE, KEYS), BF16)),
        in_specs=[vmem] * 4,
        out_specs=[pl.BlockSpec(memory_space=pl.ANY)] * 2,
        scratch_shapes=[
            pltpu.VMEM((2, HEADS_HERE, SLAB, KEYS), BF16),
            pltpu.VMEM((4, CHUNK * 8, 128), F32),
            pltpu.VMEM((LATENTS // CHUNK, CHUNK, HEADS_HERE, KEYS), BF16),
            pltpu.SemaphoreType.DMA((6,)),
            pltpu.SemaphoreType.DMA((2,)),
            pltpu.SemaphoreType.DMA((LATENTS // CHUNK,)),
        ],
        compiler_params=pltpu.CompilerParams(vmem_limit_bytes=24 << 20),
    )(done, uq, ukt, p)


def shards(changed_layers, bucket_owner, query_up, key_up, query_latent):
    done, uq, ukt, p = gather(changed_layers, bucket_owner, query_up.transpose(1, 0, 2), key_up, query_latent)
    absorbed, projected = expand(done, uq, ukt, p)
    return absorbed[None], projected[None]


def solution(mesh):
    in_specs = (
        P(),
        P(),
        P(None, ("replica", "tp"), None),
        P(None, ("replica", "tp"), None),
        P("replica", None),
    )
    out_specs = (P(None, "tp", None, None), P(None, "replica", "tp", None))
    return jax.shard_map(shards, mesh=mesh, in_specs=in_specs, out_specs=out_specs, check_vma=False)
```

time: 323 us -> 59.6 us (0.18); the launches traced: 317 us -> 59.5 us
  waiting for transfers between devices: 173 us -> 0 us
  Pallas kernels: 0 us -> 58.7 us
  local copies, waits for them, and re-layouts: 52.7 us -> 0 us
  matrix products: 36.4 us -> 0 us
  other arithmetic: 30.1 us -> 0 us
  between operations: 16.2 us -> 0.8 us
  starting transfers between devices: 9.25 us -> 0 us
    all_gather x2 -> x0, waiting for transfers between devices: 141 us -> none  [the longest x1 87.7 us: shards(): query_all = lax.all_gather(up_query, 'replica', axis=0, tiled=True)]
    pallas_call x0 -> x2, Pallas kernels: none -> 58.7 us  [the longest x1 50.8 us: gather(): pl.pallas_call(gather_kernel, out_shape=(pltpu.VMEM((HEADS_HERE, QUERIES,...]
    dot_general x9 -> x0, matrix products: 36.4 us -> none  [the longest x8 21.7 us: one_head(): lax.dot_general(pair[0], pair[1], (((1,), (1,)), ((), ())), preferred_ele...]
    all_to_all x2 -> x0, waiting for transfers between devices: 31.4 us -> none  [the longest x1 31.4 us: shards(): lax.all_to_all(query_all, 'tp', split_axis=1, concat_axis=0, tiled=True)]
    all_gather x2 -> x0, other arithmetic: 27.7 us -> none  [the longest x1 19.9 us: shards(): query_all = lax.all_gather(up_query, 'replica', axis=0, tiled=True)]
    unnamed x8 -> x0, local copies, waits for them, and re-layouts: 10.2 us -> none
    all_to_all x4 -> x0, local copies, waits for them, and re-layouts: 9.28 us -> none  [the longest x2 7.63 us: shards(): lax.all_to_all(query_all, 'tp', split_axis=1, concat_axis=0, tiled=True)]
    all_to_all x2 -> x0, starting transfers between devices: 9.17 us -> none  [the longest x1 4.79 us: shards(): lax.all_to_all(query_all, 'tp', split_axis=1, concat_axis=0, tiled=True)]
  transfers between devices with their start and end apart: 4 -> 0, of which waited for: 3 -> 0; matrix products, arithmetic and copies ran while one was open for 14% -> 0% of each run, Pallas kernels for 0% -> 0%
where the time goes in v2:
time: 59.6 us; the launch traced here: 59.5 us
  Pallas kernels  58.7 us (98%)
  between operations  0.8 us (1%)
    pallas_call x1, Pallas kernels, gather(): pl.pallas_call(gather_kernel, out_shape=(pltpu.VMEM((HEADS_HERE, QUERIES,...  50.8 us
    pallas_call x1, Pallas kernels, expand(): pl.pallas_call(expand_kernel, out_shape=(jax.ShapeDtypeStruct((HEADS_HERE...  7.83 us

profile of v2, /device:TPU:0, one launch (start us, length us, event | category | flops | bytes accessed | tf_op | source)
XLA Modules:
  0.0 59.5 jit_solution(15895458039055097927)
XLA Ops:
  0.6 50.8 %shard_map.68 = (bf16[8,1536,512]{2,1,0:T(8,128)(2,1)S(1)}, bf16[2,192,1024]{2,1,0:T(8,128)(2,1)S(1)}, bf16[8,128,512]{2,1,0:T(8,128)(2,1)S(1)}, bf16[768,1024]{1,0:T(8,128)(2,1)S(1)}) custom-call(s32[4]{0:T(128)} %layer_hbm.1, s32[16]{0:T(128)} %owner_hbm.1, bf16[12,4,16384]{2,1,0:T(4,128)(2,1)} %bitcast.3, bf16[4,4,16384]{2,1,0:T(4,128)(2,1)} %k_hbm.1, ...), custom_call_target="tpu_custom_call" | custom-call | tf_op jit(solution)/shard_map/pallas_call | solution.py:358
  51.5 7.8 %shard_map.69 = (bf16[8,1536,512]{2,1,0:T(8,128)(2,1)}, bf16[768,8,512]{2,1,0:T(8,128)(2,1)}) custom-call(bf16[8,1536,512]{2,1,0:T(8,128)(2,1)S(1)} %get-tuple-element.8.done_ref, bf16[2,192,1024]{2,1,0:T(8,128)(2,1)S(1)} %get-tuple-element.9.uq_ref, bf16[8,128,512]{2,1,0:T(8,128)(2,1)S(1)} %get-tuple-element.10.ukt_ref, ...), custom_call_target="tpu_custom_call" | custom-call | tf_op jit(solution)/shard_map/pallas_call | solution.py:424

commit v3 on v2

--- a/solution.py
+++ b/solution.py
@@ -310,16 +310,17 @@
     query_slab(0, 0, first=True)
     for n in range(4):
         row_on(3, n)
+    for n in range(4):
+        arrive(queries(0, 1, n), q_sem.at[1, 0, n])
+    query_slab(0, 1)
     hand_across(0)
     for n in range(4):
         row_on(2, n)
     hand_across(1)
     query_slab(1, 0)
-    for dz in (1, 3):
-        row = 0 if dz == 1 else 1
-        for n in range(4):
-            arrive(queries(row, dz, n), q_sem.at[dz, row, n])
-        query_slab(0, dz)
+    for n in range(4):
+        arrive(queries(1, 3, n), q_sem.at[3, 1, n])
+    query_slab(0, 3)
     for dz in (1, 3):
         for row in range(4):
             if (row, dz) not in ((0, 3), (1, 1)):

time: 59.6 us -> 58 us (0.973)
  Pallas kernels: 58.7 us -> 57.1 us
    pallas_call x1, Pallas kernels: 50.8 us -> 49.3 us  [gather(): pl.pallas_call(gather_kernel, out_shape=(pltpu.VMEM((HEADS_HERE, QUERIES,...]
where the time goes in v3:
time: 58 us; the launch traced here: 57.9 us
  Pallas kernels  57.1 us (98%)
  between operations  0.8 us (1%)
    pallas_call x1, Pallas kernels, gather(): pl.pallas_call(gather_kernel, out_shape=(pltpu.VMEM((HEADS_HERE, QUERIES,...  49.3 us
    pallas_call x1, Pallas kernels, expand(): pl.pallas_call(expand_kernel, out_shape=(jax.ShapeDtypeStruct((HEADS_HERE...  7.83 us

profile of v3, /device:TPU:0, one launch (start us, length us, event | category | flops | bytes accessed | tf_op | source)
XLA Modules:
  0.0 57.9 jit_solution(17462080061705990323)
XLA Ops:
  0.6 49.3 %shard_map.68 = (bf16[8,1536,512]{2,1,0:T(8,128)(2,1)S(1)}, bf16[2,192,1024]{2,1,0:T(8,128)(2,1)S(1)}, bf16[8,128,512]{2,1,0:T(8,128)(2,1)S(1)}, bf16[768,1024]{1,0:T(8,128)(2,1)S(1)}) custom-call(s32[4]{0:T(128)} %layer_hbm.1, s32[16]{0:T(128)} %owner_hbm.1, bf16[12,4,16384]{2,1,0:T(4,128)(2,1)} %bitcast.3, bf16[4,4,16384]{2,1,0:T(4,128)(2,1)} %k_hbm.1, ...), custom_call_target="tpu_custom_call" | custom-call | tf_op jit(solution)/shard_map/pallas_call | solution.py:359
  49.9 7.8 %shard_map.69 = (bf16[8,1536,512]{2,1,0:T(8,128)(2,1)}, bf16[768,8,512]{2,1,0:T(8,128)(2,1)}) custom-call(bf16[8,1536,512]{2,1,0:T(8,128)(2,1)S(1)} %get-tuple-element.8.done_ref, bf16[2,192,1024]{2,1,0:T(8,128)(2,1)S(1)} %get-tuple-element.9.uq_ref, bf16[8,128,512]{2,1,0:T(8,128)(2,1)S(1)} %get-tuple-element.10.ukt_ref, ...), custom_call_target="tpu_custom_call" | custom-call | tf_op jit(solution)/shard_map/pallas_call | solution.py:425
